TPU v7x, 256 devices: a whole 4x4x8 slice. The times are simulated.
256 devices in a mesh: pipe: 4 (over y), dp: 32 (over z, x_hi, core), tensor: 2 (over x_lo).
Axes of the slice: x: 4 (x_hi: 2, x_lo: 2; x = x_hi * 2 + x_lo), y: 4, z: 8, core: 2. Of those that a mesh axis runs over, the one named last changes fastest.
Arguments:
- section_out: bfloat16 [4, 4096, 16384], P('pipe', 'dp', 'tensor'), may hold values from -6 to 6
- saved_stream: bfloat16 [4, 4096, 16384], P('pipe', 'dp', 'tensor'), may hold values from -6 to 6
- section_grad: bfloat16 [4, 4096, 16384], P('pipe', 'dp', 'tensor'), may hold values from -0.59765625 to 0.59765625
- key_grad: bfloat16 [4, 4096, 512], P('pipe', ('dp', 'tensor')), may hold values from -3 to 3
- key_weight: bfloat16 [4, 16384, 512], P('pipe', 'tensor'), may hold values from -0.09375 to 0.09375
- adapter_in: bfloat16 [4, 16384, 64], P('pipe', 'tensor'), may hold values from -0.046875 to 0.046875
- adapter_out: bfloat16 [4, 64, 512], P('pipe'), may hold values from -0.75 to 0.75
- magnitude: float32 [4, 512], P('pipe'), may hold values from 0.5 to 2
Outputs:
- projected_keys: bfloat16 [4, 4096, 512], P('pipe', ('dp', 'tensor'))
- stream_grad: bfloat16 [4, 4096, 16384], P('pipe', 'dp', 'tensor')
- magnitude_grad: float32 [4, 512], P('pipe')
- adapter_out_grad: float32 [4, 64, 512], P('pipe', None, 'dp')
- adapter_in_grad: float32 [4, 16384, 64], P('pipe', ('tensor', 'dp'))
All inputs are finite; a program needn't handle non-finite values.
Results may differ from a plain program's by a relative error of at most 0.0041.
Values may be sent and summed in bfloat16 or wider, within the bound.
A program may use at most 128 MiB of HBM per device.

v0:
```python
import jax
import jax.numpy as jnp
from jax import lax
from jax.sharding import PartitionSpec as P

EPSILON = 1e-06
HIGHEST_MODE = lax.Precision.HIGHEST


def shifted(value, axis, steps):
    count = lax.axis_size(axis)
    pairs = [(source, (source + steps) % count) for source in range(count)]
    return lax.ppermute(value, axis, pairs)


def contract_rows(left_side, right_side, precision_mode=None):
    return lax.dot_general(
        left_side,
        right_side,
        (((0,), (0,)), ((), ())),
        precision=precision_mode,
        preferred_element_type=jnp.float32,
    )


def contract_cols(left_side, right_side, precision_mode=None):
    return lax.dot_general(
        left_side,
        right_side,
        (((1,), (1,)), ((), ())),
        precision=precision_mode,
        preferred_element_type=jnp.float32,
    )


def project(stream, weight, adapt_in, up_wide):
    low_part = jnp.dot(stream, adapt_in, preferred_element_type=jnp.float32)
    raw_part = jnp.dot(stream, weight, preferred_element_type=jnp.float32) + jnp.dot(
        low_part, up_wide, precision=HIGHEST_MODE
    )
    return (raw_part, low_part)


def split_product(narrow_left, wide_right):
    upper_part = wide_right.astype(jnp.bfloat16)
    lower_part = (wide_right - upper_part.astype(jnp.float32)).astype(jnp.bfloat16)
    return jnp.dot(narrow_left, upper_part, preferred_element_type=jnp.float32) + jnp.dot(
        narrow_left, lower_part, preferred_element_type=jnp.float32
    )


def per_device(
    section_out,
    saved_stream,
    section_grad,
    key_grad,
    key_weight,
    adapter_in,
    adapter_out,
    magnitude,
):
    weight = key_weight[0]
    adapt_in = adapter_in[0]
    adapt_out = adapter_out[0]
    up_wide = adapt_out.astype(jnp.float32)
    magnitudes = magnitude[0]
    forward_stream = shifted(section_out[0], "pipe", 1)
    cross_low = contract_rows(adapt_in, weight)
    gram_low = contract_rows(adapt_in, adapt_in)
    gram_up = jnp.dot(gram_low, up_wide, precision=HIGHEST_MODE)
    cross_part = cross_low + gram_up
    combined = weight.astype(jnp.float32) + jnp.dot(
        adapt_in, adapt_out, preferred_element_type=jnp.float32
    )
    square_part = jnp.sum(combined * combined, axis=0)
    square_total, cross_total = lax.psum((square_part, cross_part), "tensor")
    key_rows = lax.psum_scatter(
        project(forward_stream, weight, adapt_in, up_wide)[0],
        "tensor",
        scatter_dimension=0,
        tiled=True,
    )
    col_norm = jnp.sqrt(square_total + EPSILON)
    col_scale = magnitudes / col_norm
    key_out = (key_rows * col_scale).astype(jnp.bfloat16)
    key_cot = lax.all_gather(key_grad[0], "tensor", axis=0, tiled=True)
    next_grad = shifted(section_grad[0], "pipe", -1)
    key_scaled = key_cot.astype(jnp.float32) * col_scale
    key_scaled_b = key_scaled.astype(jnp.bfloat16)
    low_grad = contract_cols(key_scaled, up_wide, HIGHEST_MODE).astype(jnp.bfloat16)
    stream_part = contract_cols(key_scaled_b, weight) + contract_cols(low_grad, adapt_in)
    stream_out = (next_grad.astype(jnp.float32) + stream_part).astype(jnp.bfloat16)
    saved_rows = saved_stream[0]
    raw_saved, low_saved = project(saved_rows, weight, adapt_in, up_wide)
    scale_part = jnp.sum(key_cot.astype(jnp.float32) * raw_saved, axis=0)
    out_part = contract_rows(low_saved, key_scaled, HIGHEST_MODE)
    scale_grad, out_direct = lax.psum((scale_part, out_part), ("dp", "tensor"))
    in_part = contract_rows(saved_rows, low_grad)
    replicas = lax.axis_size("dp")
    position = lax.axis_index("dp")
    factor = -scale_grad * magnitudes / (col_norm * col_norm * col_norm)
    mag_grad = scale_grad / col_norm / replicas
    out_grad = (out_direct + cross_total * factor) / replicas
    col_share = out_grad.shape[1] // replicas
    out_share = lax.dynamic_slice_in_dim(out_grad, position * col_share, col_share, 1)
    turned = factor[:, None] * up_wide.T
    small_turned = jnp.dot(up_wide, turned, precision=HIGHEST_MODE)
    row_share = weight.shape[0] // replicas
    in_summed = lax.psum(in_part, "dp")
    in_full = (
        in_summed
        + (
            split_product(weight, turned)
            + jnp.dot(adapt_in.astype(jnp.float32), small_turned, precision=HIGHEST_MODE)
        )
    ) / replicas
    in_share = lax.dynamic_slice_in_dim(in_full, position * row_share, row_share, 0)
    return (key_out[None], stream_out[None], mag_grad[None], out_share[None], in_share[None])


def solution(mesh):
    placed = (
        P("pipe", "dp", "tensor"),
        P("pipe", "dp", "tensor"),
        P("pipe", "dp", "tensor"),
        P("pipe", ("dp", "tensor"), None),
        P("pipe", "tensor", None),
        P("pipe", "tensor", None),
        P("pipe", None, None),
        P("pipe", None),
    )
    return jax.shard_map(
        per_device,
        mesh=mesh,
        in_specs=placed,
        out_specs=(
            P("pipe", ("dp", "tensor"), None),
            P("pipe", "dp", "tensor"),
            P("pipe", None),
            P("pipe", None, "dp"),
            P("pipe", ("tensor", "dp"), None),
        ),
        check_vma=False,
    )
```

profile of v0, /device:TPU:64, one launch (start us, length us, event | category | flops | bytes accessed | tf_op | source)
XLA Modules:
  0.0 670.2 jit_solution(10722553665710226972)
XLA Ops:
  7.2 5.3 all-gather
  12.5 2.2 fusion.14
  14.8 4.8 fusion.6
  19.6 2.5 multiply_reduce_fusion
  22.1 0.3 fusion.21
  22.5 106.2 %psum.36 = f32[512]{0:T(512)S(1)} all-reduce(f32[512]{0:T(512)S(1)} %fusion.21), channel_id=1, replica_groups=mesh['pipe'=4,'dp'=32,'tensor'=2] {'dp','tensor'}, use_global_device_ids=true, to_apply=%region_4.0 | all-reduce | flops 512 | bytes 4096 | tf_op jit(solution)/shard_map/psum | solution.py:97
  128.6 4.9 psum.35
  133.6 0.6 fusion.63
  134.2 1.3 fusion.33
  135.5 3.1 collective-permute-start.1
  138.7 6.7 %fusion.4 = f32[64,512]{0,1:T(8,128)S(1)} fusion(bf16[1,8192,512]{2,1,0:T(8,128)(2,1)} %param.12, bf16[1,8192,64]{1,2,0:T(8,128)(2,1)S(1)} %copy-done.1), kind=kOutput, calls=%fused_computation.9 | convolution fusion | flops 536870912 | bytes 9568256 | tf_op jit(solution)/shard_map/dot_general | solution.py:17
  145.4 0.4 fusion.23
  145.8 1.0 convolution_add_fusion.3
  146.9 0.3 convolution_convert_fusion
  147.2 1.7 convolution_bitcast_fusion
  149.0 0.2 reduce-scatter.2.cloned.1.call-start
  149.3 6.2 fusion.2
  155.5 0.5 fusion.36
  156.0 6.2 convolution_add_fusion.2
  162.2 2.4 fusion
  164.6 8.2 %fusion.8 = f32[128,8192]{1,0:T(8,128)} fusion(bf16[1,8192,512]{2,1,0:T(8,128)(2,1)} %param.12, bf16[1,128,512]{2,1,0:T(8,128)(2,1)S(1)} %all-gather, f32[512]{0:T(512)S(1)} %get-tuple-element.7), kind=kOutput, calls=%fused_computation.13 | convolution fusion | flops 1073938432 | bytes 12716032 | tf_op jit(solution)/shard_map/dot_general | solution.py:27
  172.8 155.7 %all-reduce.4.cloned.1.call-done = f32[64,512]{0,1:T(8,128)} async-done(((f32[64,512]{0,1:T(8,128)}), f32[64,512]{0,1:T(8,128)}) %all-reduce.4.cloned.1.call-update) | async-done | bytes 131088 | tf_op jit(solution)/shard_map/psum | solution.py:97
  328.5 38.0 %all-reduce.6.cloned.1.call-done = f32[64,512]{0,1:T(8,128)} async-done(((f32[64,512]{0,1:T(8,128)}), f32[64,512]{0,1:T(8,128)}) %all-reduce.6.cloned.1.call-update) | async-done | bytes 131088 | tf_op jit(solution)/shard_map/psum | solution.py:76
  366.5 1.4 fusion.62
  367.9 2.3 fusion.29
  370.2 0.2 fusion.59
  370.5 6.0 fusion.18
  376.5 257.6 %all-reduce.8.cloned.1.call-done = f32[8192,64]{0,1:T(8,128)} async-done(((f32[8192,64]{0,1:T(8,128)}), f32[8192,64]{0,1:T(8,128)}) %all-reduce.8.cloned.1.call-update) | async-done | bytes 2097168 | tf_op jit(solution)/shard_map/psum | solution.py:109
  634.0 1.5 fusion.53
  635.6 4.9 fusion.12
  640.4 21.7 %reduce-scatter.2.cloned.1.call-done = f32[64,512]{1,0:T(8,128)} async-done(((f32[128,512]{1,0:T(8,128)}), f32[64,512]{1,0:T(8,128)}) %reduce-scatter.2.cloned.1.call-update) | async-done | bytes 131088 | tf_op jit(solution)/shard_map/reduce_scatter | solution.py:77
  662.1 1.5 fusion.51
  (25 shorter events, 0.4 us)
Async XLA Ops:
  7.2 5.3 copy-start
  7.2 321.3 %all-reduce.4.cloned.1.call-start = ((), (), s32[]{:S(2)}) async-start(), calls=%async_computation.2 | async-start | bytes 524288 | tf_op jit(solution)/shard_map/psum | solution.py:97
  12.5 7.1 %slice-start = ((s8[8388608]{0:T(1024)(128)(4,1)}), s8[4194304]{0:T(1024)(128)(4,1)S(1)}, s32[]{:S(2)}) async-start(s8[8388608]{0:T(1024)(128)(4,1)} %bitcast.120), calls=%async_computation.5 | async-start | bytes 8388608
  14.7 4.8 slice-start.1
  14.8 4.9 copy-start.1
  14.8 4.9 copy-start.2
  19.6 114.0 %copy-start.3 = (f32[1,512]{1,0:T(1,128)S(1)}, f32[1,512]{1,0:T(1,128)}, u32[]{:S(2)}) copy-start(f32[1,512]{1,0:T(1,128)} %param.15) | copy-start | bytes 6148
  135.5 231.0 %all-reduce.6.cloned.1.call-start = ((), (), s32[]{:S(2)}) async-start(), calls=%async_computation.3 | async-start | bytes 524288 | tf_op jit(solution)/shard_map/psum | solution.py:76
  135.5 500.0 %collective-permute-start.1 = (bf16[128,8192]{1,0:T(8,128)(2,1)}, bf16[128,8192]{1,0:T(8,128)(2,1)}, u32[]{:S(2)}, u32[]{:S(2)}) collective-permute-start(bf16[128,8192]{1,0:T(8,128)(2,1)} %bitcast.125), channel_id=1, source_target_pairs={{0,192},{64,0},{128,64},{192,128},{1,193},{65,1},{129,65},{193,129... | collective-permute-start | bytes 6291464 | tf_op jit(solution)/shard_map/ppermute | solution.py:13
  138.7 229.3 %collective-permute-start = (bf16[128,8192]{1,0:T(8,128)(2,1)}, bf16[128,8192]{1,0:T(8,128)(2,1)}, u32[]{:S(2)}, u32[]{:S(2)}) collective-permute-start(bf16[128,8192]{1,0:T(8,128)(2,1)} %bitcast.124), channel_id=1, source_target_pairs={{0,64},{64,128},{128,192},{192,0},{1,65},{65,129},{129,193},{193,1... | collective-permute-start | bytes 6291464 | tf_op jit(solution)/shard_map/ppermute | solution.py:13
  146.9 487.2 %all-reduce.8.cloned.1.call-start = ((), (), s32[]{:S(2)}) async-start(), calls=%async_computation.4 | async-start | bytes 4194304 | tf_op jit(solution)/shard_map/psum | solution.py:109
  149.0 513.1 %reduce-scatter.2.cloned.1.call-start = ((), (), s32[]{:S(2)}) async-start(), calls=%async_computation.1 | async-start | bytes 393216 | tf_op jit(solution)/shard_map/reduce_scatter | solution.py:77
Sparse Core Ops, SparseCore 0:
  135.6 192.8 all-reduce.3
  331.3 35.2 all-reduce.5
  369.2 264.8 all-reduce.7
  636.5 25.5 reduce-scatter.1
where the time goes:
time: 672 us; the launch traced here: 670 us
  waiting for transfers between devices  473 us (70%)
  blocking collectives  116 us (17%)
  matrix products  58.1 us (9%)
  between operations  13.9 us (2%)
    psum x1, waiting for transfers between devices, per_device(): in_summed = lax.psum(in_part, 'dp')  258 us
    psum x1, waiting for transfers between devices, per_device(): scale_grad, out_direct = lax.psum((scale_part, out_part), ('dp', 'tensor'))  156 us
    psum x1, blocking collectives, per_device(): scale_grad, out_direct = lax.psum((scale_part, out_part), ('dp', 'tensor'))  106 us
    psum x1, waiting for transfers between devices, per_device(): square_total, cross_total = lax.psum((square_part, cross_part), 'tensor')  38 us
    reduce_scatter x1, waiting for transfers between devices, per_device(): lax.psum_scatter(project(forward_stream, weight, adapt_in, up_wide)[0], '...  21.7 us
  transfers between devices with their start and end apart: 6, of which 4 were waited for; matrix products, arithmetic and copies ran while one was open for 7% of the time, Pallas kernels for 0%

commit v1 on v0

v1 whole, which is shorter than its diff:
```python
import jax
import jax.numpy as jnp
from jax import lax
from jax.experimental import pallas as pl
from jax.experimental.pallas import tpu as pltpu
from jax.sharding import PartitionSpec as P

EPSILON = 1e-06
MESH = pl.DeviceIdType.MESH
BF = jnp.bfloat16
F32 = jnp.float32

PIPES = 4
REPLICAS = 32
RINGS = 8
TOK = 128
HALF = 64
COLS = 512
RANK = 64
FEAT = 8192
SHARE = FEAT // REPLICAS
OUTROWS = COLS // REPLICAS
DEPTH = 512
FWD_PIECES = 4
GRAD_PIECES = 8


def mm(left, right, left_dim, right_dim):
    return lax.dot_general(
        left, right, (((left_dim,), (right_dim,)), ((), ())), preferred_element_type=F32
    )


def halves(value):
    upper = value.astype(BF)
    lower = (value - upper.astype(F32)).astype(BF)
    return upper, lower


def mm2(wide, narrow, left_dim, right_dim):
    upper, lower = halves(wide)
    return mm(upper, narrow, left_dim, right_dim) + mm(lower, narrow, left_dim, right_dim)


def kernel(
    x, sv, sg, kg, w, bt, a, mag,
    keys, so, mg, og, ig,
    wv, lv, fw, gr, st, sp, kc, raw, low, sq, sqr, ksb, lgv, fac, flo,
    ox, oxr, o2, o2r, o3, o3r, o4, o4r,
    s0, s0r, s1, s1r, zs, s3, s3r,
    ind, ra, sb, rb, c0, rc, fp, fpr, cv,
    loc, outs, fs, fr, gs, gf, ts, tr, cs, cr, zsd, zrv, hs, hr,
):
    p = lax.axis_index("pipe")
    d = lax.axis_index("dp")
    t = lax.axis_index("tensor")
    z, h, c = d // 4, (d // 2) % 2, d % 2

    def dev(p_=p, z_=z, h_=h, c_=c, t_=t):
        return {"pipe": p_, "dp": (z_ * 2 + h_) * 2 + c_, "tensor": t_}

    up, down = dev(p_=(p + 1) % PIPES), dev(p_=(p + PIPES - 1) % PIPES)
    pair, mate, across = dev(t_=1 - t), dev(c_=1 - c), dev(h_=1 - h)
    ring = [dev(z_=(z + k) % RINGS) for k in range(1, RINGS)]

    def remote(src, dst, ssem, rsem, to):
        cp = pltpu.make_async_remote_copy(
            src_ref=src, dst_ref=dst, send_sem=ssem, recv_sem=rsem, device_id=to, device_id_type=MESH
        )
        cp.start()
        return cp

    locals_ = [
        pltpu.make_async_copy(kg, kc.at[t], loc.at[0]),
        pltpu.make_async_copy(sv, lv.at[pl.ds(0, TOK)], loc.at[1]),
        pltpu.make_async_copy(bt, lv.at[pl.ds(TOK, RANK)], loc.at[2]),
    ]
    for i in range(4):
        rows = pl.ds(i * (FEAT // 4), FEAT // 4)
        locals_.append(pltpu.make_async_copy(w.at[rows], wv.at[rows], loc.at[3 + i]))
    for cp in locals_:
        cp.start()

    barrier = pltpu.get_barrier_semaphore()
    peers = [up, down, pair, mate, across] + ring
    for to in peers:
        pl.semaphore_signal(barrier, inc=1, device_id=to, device_id_type=MESH)
    pl.semaphore_wait(barrier, len(peers))

    kcp = remote(kg, kc.at[t], ts.at[0], tr.at[0], pair)
    fwd, grad = [], []
    wide = FEAT // FWD_PIECES
    narrow = FEAT // GRAD_PIECES
    for i in range(GRAD_PIECES):
        j = i % FWD_PIECES
        rows = pl.ds(pl.multiple_of((1 - t if i < FWD_PIECES else t) * HALF, HALF), HALF)
        at = (rows, pl.ds(j * wide, wide))
        fwd.append(remote(x.at[at], fw.at[at], fs.at[i], fr.at[i], up))
        at = (slice(None), pl.ds(i * narrow, narrow))
        grad.append(remote(sg.at[at], gr.at[at], gs.at[i], gf.at[i], down))

    raw[...] = jnp.zeros_like(raw)
    low[...] = jnp.zeros_like(low)
    sq[...] = jnp.zeros_like(sq)
    for cp in locals_:
        cp.wait()

    @pl.loop(0, FEAT // DEPTH)
    def _(i):
        part = pl.ds(pl.multiple_of(i * DEPTH, DEPTH), DEPTH)
        left = lv[:, part]
        wc = wv[part, :]
        bc = lv[pl.ds(TOK, RANK), part]
        raw[...] += mm(left, wc, 1, 0)
        low[...] += mm(left, bc, 1, 1)
        combined = wc.astype(F32) + mm(bc, a[...], 0, 0)
        sq[...] += jnp.sum((combined * combined).reshape(DEPTH // 8, 8, COLS), axis=0)

    sqc = remote(sq, sqr, ts.at[1], tr.at[1], pair)

    av = a[...]
    lows = low[pl.ds(0, TOK), :]
    lhi, llo = halves(lows)
    raw_saved = raw[pl.ds(0, TOK), :] + mm(lhi, av, 1, 0) + mm(llo, av, 1, 0)
    kcp.wait_recv()
    cot = kc[...].reshape(TOK, COLS)
    cot32 = cot.astype(F32)
    s0[...] = jnp.sum((cot32 * raw_saved).reshape(TOK // 8, 8, COLS), axis=0)
    s0c = remote(s0, s0r, ts.at[2], tr.at[2], pair)
    ox[:, pl.ds(0, RANK)] = mm(cot, lhi, 0, 0) + mm(cot, llo, 0, 0)
    cross = raw[pl.ds(TOK, RANK), :] + mm2(low[pl.ds(TOK, RANK), :], av, 1, 0)
    ox[:, pl.ds(RANK, RANK)] = cross.T
    oxc = remote(ox, oxr, ts.at[3], tr.at[3], pair)

    sqc.wait_recv()
    norm = jnp.sqrt(jnp.sum(sq[...] + sqr[...], axis=0, keepdims=True) + EPSILON)
    scale = mag[...] / norm
    scaled = cot32 * scale
    shi, slo = halves(scaled)
    ksb[...] = shi
    low_grad = mm(shi, av, 1, 1) + mm(slo, av, 1, 1)
    lgv[...] = low_grad.astype(BF)
    turned_grad = low_grad.T.astype(BF)

    @pl.loop(0, REPLICAS // 2)
    def _(i):
        for k in range(2):
            part = pl.ds(pl.multiple_of((i * 2 + k) * SHARE, SHARE), SHARE)
            ind[k, i] = mm(turned_grad, lv[pl.ds(0, TOK), part], 1, 0)

    indc = remote(ind.at[1 - c], ra, cs.at[0], cr.at[0], mate)

    s0c.wait_recv()
    s1[...] = s0[...] + s0r[...]
    s1c = remote(s1, s1r, cs.at[1], cr.at[1], mate)
    oxc.wait_recv()
    both = (ox[...] + oxr[...]).reshape(REPLICAS // 2, 2, OUTROWS, 2 * RANK)
    o2[0] = both[:, 0]
    o2[1] = both[:, 1]
    o2c = remote(o2.at[1 - c], o2r, cs.at[2], cr.at[2], mate)

    def stream_piece(i):
        part = pl.ds(pl.multiple_of(i * narrow, narrow), narrow)
        sp[:, part] = mm(ksb[...], wv[part, :], 1, 1) + mm(lgv[...], lv[pl.ds(TOK, RANK), part], 1, 0)

    pl.loop(0, GRAD_PIECES // 2)(stream_piece)

    s1c.wait_recv()
    zs[z] = s1[...] + s1r[...]
    zsc = [remote(zs.at[z], zs.at[z], zsd.at[k], zrv.at[k], to) for k, to in enumerate(ring)]
    o2c.wait_recv()
    o3[...] = (o2[c] + o2r[...]).reshape(RINGS, 2, OUTROWS, 2 * RANK)
    o3c = [
        remote(o3.at[(z + k + 1) % RINGS], o3r.at[z], zsd.at[7 + k], zrv.at[7 + k], to)
        for k, to in enumerate(ring)
    ]
    indc.wait_recv()

    @pl.loop(0, RINGS)
    def _(i):
        for k in range(2):
            sb[i, k] = (ind[c, i * 2 + k] + ra[i * 2 + k]).astype(BF)

    sbc = [
        remote(sb.at[(z + k + 1) % RINGS], rb.at[z], zsd.at[14 + k], zrv.at[14 + k], to)
        for k, to in enumerate(ring)
    ]

    pl.loop(GRAD_PIECES // 2, GRAD_PIECES)(stream_piece)

    writes = []

    def finish_grad(i):
        grad[i].wait_recv()
        at = (slice(None), pl.ds(i * narrow, narrow))
        st[at] = (sp[at] + gr[at].astype(F32)).astype(BF)
        cp = pltpu.make_async_copy(st.at[at], so.at[at], outs.at[i])
        cp.start()
        writes.append(cp)

    def take_forward(i):
        fwd[i].wait_recv()
        j = i % FWD_PIECES
        rows = pl.ds(pl.multiple_of((1 - t if i < FWD_PIECES else t) * HALF, HALF), HALF)
        if j == 0:
            fac[...] = jnp.zeros_like(fac)
            flo[...] = jnp.zeros_like(flo)

        @pl.loop(0, wide // DEPTH)
        def _(k):
            part = pl.ds(pl.multiple_of(j * wide + k * DEPTH, DEPTH), DEPTH)
            rowsv = fw[rows, part]
            fac[...] += mm(rowsv, wv[part, :], 1, 0)
            flo[...] += mm(rowsv, lv[pl.ds(TOK, RANK), part], 1, 1)

    def partial_keys():
        return fac[...] + mm2(flo[...], a[...], 1, 0)

    for i in range(FWD_PIECES):
        take_forward(i)
        finish_grad(i)
    fp[...] = partial_keys()
    fpc = remote(fp, fpr, ts.at[4], tr.at[4], pair)

    for cp in zsc:
        cp.wait_recv()
    total = zs[0]
    for k in range(1, RINGS):
        total = total + zs[k]
    s3[...] = total
    s3c = remote(s3, s3r, hs.at[0], hr.at[0], across)
    for cp in o3c:
        cp.wait_recv()
    total = o3[z]
    for k in range(1, RINGS):
        total = total + o3r[(z + k) % RINGS]
    o4[...] = total
    o4c = remote(o4.at[1 - h], o4r, hs.at[1], hr.at[1], across)

    take_forward(4)
    finish_grad(4)
    for cp in sbc:
        cp.wait_recv()
    for k in range(2):
        total = ind[c, z * 2 + k] + ra[z * 2 + k]
        for n in range(1, RINGS):
            total = total + rb[(z + n) % RINGS, k].astype(F32)
        c0[k] = total
    c0c = remote(c0.at[1 - h], rc, hs.at[2], hr.at[2], across)

    take_forward(5)
    finish_grad(5)
    s3c.wait_recv()
    scale_grad = jnp.sum(s3[...] + s3r[...], axis=0, keepdims=True)
    factor = -scale_grad * mag[...] / (norm * norm * norm)
    mg[...] = scale_grad / norm / REPLICAS
    columns = jnp.concatenate([scale, factor, jnp.zeros((6, COLS), F32)], axis=0)
    cv[...] = columns.T
    o4c.wait_recv()
    mine = pl.ds(pl.multiple_of(d * OUTROWS, OUTROWS), OUTROWS)
    direct = o4[h][:, :RANK] + o4r[:, pl.ds(0, RANK)]
    shared = o2[c, z * 2 + h][:, RANK:]
    og[...] = (direct * cv[mine, pl.ds(0, 1)] + shared * cv[mine, pl.ds(1, 1)]) / REPLICAS
    turned = a[...].astype(F32) * factor
    thi, tlo = halves(turned)
    part = pl.ds(pl.multiple_of(d * SHARE, SHARE), SHARE)
    wsh = wv[part, :]
    small = mm(thi, a[...], 1, 1) + mm(tlo, a[...], 1, 1)
    term = mm(thi, wsh, 1, 1) + mm(tlo, wsh, 1, 1) + mm2(small, lv[pl.ds(TOK, RANK), part], 1, 0)

    take_forward(6)
    finish_grad(6)
    c0c.wait_recv()
    ig[...] = (c0[h] + rc[...] + term) / REPLICAS
    fpc.wait_recv()

    take_forward(7)
    keys[...] = ((partial_keys() + fpr[...]) * scale).astype(BF)
    finish_grad(7)

    for cp in [kcp, sqc, s0c, oxc, indc, s1c, o2c, fpc, s3c, o4c, c0c] + zsc + o3c + sbc + fwd + grad:
        cp.wait_send()
    for cp in writes:
        cp.wait()


def per_device(section_out, saved_stream, section_grad, key_grad, key_weight, adapter_in, adapter_out, magnitude):
    vmem = pl.BlockSpec(memory_space=pltpu.VMEM)
    hbm = pl.BlockSpec(memory_space=pl.ANY)
    dma = pltpu.SemaphoreType.DMA
    V = pltpu.VMEM
    half = REPLICAS // 2
    keys, so, mg, og, ig = pl.pallas_call(
        kernel,
        out_shape=[
            jax.ShapeDtypeStruct((HALF, COLS), BF),
            jax.ShapeDtypeStruct((TOK, FEAT), BF),
            jax.ShapeDtypeStruct((1, COLS), F32),
            jax.ShapeDtypeStruct((OUTROWS, RANK), F32),
            jax.ShapeDtypeStruct((RANK, SHARE), F32),
        ],
        in_specs=[hbm] * 6 + [vmem] * 2,
        out_specs=[vmem, hbm, vmem, vmem, vmem],
        scratch_shapes=[
            V((FEAT, COLS), BF),
            V((TOK + RANK, FEAT), BF),
            V((TOK, FEAT), BF),
            V((TOK, FEAT), BF),
            V((TOK, FEAT), BF),
            V((TOK, FEAT), F32),
            V((2, HALF, COLS), BF),
            V((TOK + RANK, COLS), F32),
            V((TOK + RANK, RANK), F32),
            V((8, COLS), F32),
            V((8, COLS), F32),
            V((TOK, COLS), BF),
            V((TOK, RANK), BF),
            V((HALF, COLS), F32),
            V((HALF, RANK), F32),
            V((COLS, 2 * RANK), F32),
            V((COLS, 2 * RANK), F32),
            V((2, half, OUTROWS, 2 * RANK), F32),
            V((half, OUTROWS, 2 * RANK), F32),
            V((RINGS, 2, OUTROWS, 2 * RANK), F32),
            V((RINGS, 2, OUTROWS, 2 * RANK), F32),
            V((2, OUTROWS, 2 * RANK), F32),
            V((OUTROWS, 2 * RANK), F32),
            V((8, COLS), F32),
            V((8, COLS), F32),
            V((8, COLS), F32),
            V((8, COLS), F32),
            V((RINGS, 8, COLS), F32),
            V((8, COLS), F32),
            V((8, COLS), F32),
            V((2, half, RANK, SHARE), F32),
            V((half, RANK, SHARE), F32),
            V((RINGS, 2, RANK, SHARE), BF),
            V((RINGS, 2, RANK, SHARE), BF),
            V((2, RANK, SHARE), F32),
            V((RANK, SHARE), F32),
            V((HALF, COLS), F32),
            V((HALF, COLS), F32),
            V((COLS, 8), F32),
            dma((7,)),
            dma((GRAD_PIECES,)),
            dma((GRAD_PIECES,)),
            dma((GRAD_PIECES,)),
            dma((GRAD_PIECES,)),
            dma((GRAD_PIECES,)),
            dma((5,)),
            dma((5,)),
            dma((3,)),
            dma((3,)),
            dma((21,)),
            dma((21,)),
            dma((3,)),
            dma((3,)),
        ],
        compiler_params=pltpu.CompilerParams(
            collective_id=0, has_side_effects=True, vmem_limit_bytes=56 * 2**20
        ),
        name="relay_tick",
    )(
        section_out[0],
        saved_stream[0],
        section_grad[0],
        key_grad[0],
        key_weight[0],
        adapter_in[0].T,
        adapter_out[0],
        magnitude,
    )
    return (keys[None], so[None], mg, og.T[None], ig.T[None])


def solution(mesh):
    placed = (
        P("pipe", "dp", "tensor"),
        P("pipe", "dp", "tensor"),
        P("pipe", "dp", "tensor"),
        P("pipe", ("dp", "tensor"), None),
        P("pipe", "tensor", None),
        P("pipe", "tensor", None),
        P("pipe", None, None),
        P("pipe", None),
    )
    return jax.shard_map(
        per_device,
        mesh=mesh,
        in_specs=placed,
        out_specs=(
            P("pipe", ("dp", "tensor"), None),
            P("pipe", "dp", "tensor"),
            P("pipe", None),
            P("pipe", None, "dp"),
            P("pipe", ("tensor", "dp"), None),
        ),
        check_vma=False,
    )
```

time: 672 us -> 67.6 us (0.10)
  the two profiles are of different devices: /device:TPU:64 before, /device:TPU:2 now
where the time goes in v1:
time: 67.6 us; the launch traced here: 67.4 us
  Pallas kernels  60.3 us (89%)
  local copies, waits for them, and re-layouts  6.42 us (9%)
    pallas_call x1, Pallas kernels, per_device(): pl.pallas_call(kernel, out_shape=[jax.ShapeDtypeStruct((HALF, COLS), BF),...  60.3 us
    unnamed x11, local copies, waits for them, and re-layouts  6.42 us

profile of v1, /device:TPU:2, one launch (start us, length us, event | category | flops | bytes accessed | tf_op | source)
XLA Modules:
  0.0 67.4 jit_solution(3841523021817873682)
XLA Ops:
  0.6 60.3 %relay_tick.1 = (bf16[64,512]{1,0:T(8,128)(2,1)}, bf16[128,8192]{1,0:T(8,128)(2,1)}, f32[1,512]{1,0:T(1,128)}, f32[16,64]{1,0:T(8,128)}, f32[64,256]{1,0:T(8,128)}) custom-call(bf16[128,8192]{1,0:T(8,128)(2,1)} %bitcast.18, bf16[128,8192]{1,0:T(8,128)(2,1)} %bitcast.19, bf16[128,8192]{1,0:T(8,128)(2,1)} %bitcast.20, bf16[64,512]{1,0:T(8,128)(2,1)} %bitcast.23, ...), custom_call_target="tpu_custom_call" | custom-call | tf_op jit(solution)/shard_map/relay_tick/pallas_call | solution.py:293
  60.9 1.5 %copy.18 = bf16[1,64,512]{2,1,0:T(8,128)(2,1)} copy(bf16[1,64,512]{2,1,0:T(8,128)(2,1)} %bitcast.26) | data formatting | bytes 131072
  62.4 0.0 copy-start.2
  62.4 0.0 copy-start.1
  62.4 0.0 copy-start
  62.4 3.1 %copy.19 = bf16[1,128,8192]{2,1,0:T(8,128)(2,1)} copy(bf16[1,128,8192]{2,1,0:T(8,128)(2,1)} %bitcast.21) | data formatting | bytes 4194304
  65.5 0.0 copy-done.2
  65.5 0.6 copy.20
  66.1 0.0 copy-done.1
  66.1 0.6 copy.21
  66.7 0.0 copy-done
  66.7 0.6 copy.22
Async XLA Ops:
  62.4 3.1 %copy-start.2 = (f32[1,512]{1,0:T(1,128)S(1)}, f32[1,512]{1,0:T(1,128)}, u32[]{:S(2)}) copy-start(f32[1,512]{1,0:T(1,128)} %get-tuple-element.22) | copy-start | bytes 6148
  62.4 3.7 %copy-start.1 = (f32[16,64]{1,0:T(8,128)S(1)}, f32[16,64]{1,0:T(8,128)}, u32[]{:S(2)}) copy-start(f32[16,64]{1,0:T(8,128)} %get-tuple-element.13) | copy-start | bytes 12292
  62.4 4.3 %copy-start = (f32[64,256]{1,0:T(8,128)S(1)}, f32[64,256]{1,0:T(8,128)}, u32[]{:S(2)}) copy-start(f32[64,256]{1,0:T(8,128)} %get-tuple-element.14) | copy-start | bytes 196612

commit v2 on v1

--- a/solution.py
+++ b/solution.py
@@ -43,13 +43,13 @@
 
 
 def kernel(
-    x, sv, sg, kg, w, bt, a, mag,
+    x, sv, sg, kg, w, bt, a_in, mag_in,
     keys, so, mg, og, ig,
-    wv, lv, fw, gr, st, sp, kc, raw, low, sq, sqr, ksb, lgv, fac, flo,
+    a, mag, wv, lv, fw, gr, sp, kc, raw, low, sq, sqr, ksb, lgv, fac, flo,
     ox, oxr, o2, o2r, o3, o3r, o4, o4r,
     s0, s0r, s1, s1r, zs, s3, s3r,
     ind, ra, sb, rb, c0, rc, fp, fpr, cv,
-    loc, outs, fs, fr, gs, gf, ts, tr, cs, cr, zsd, zrv, hs, hr,
+    loc, fs, fr, gs, gf, ts, tr, cs, cr, zsd, zrv, hs, hr, know,
 ):
     p = lax.axis_index("pipe")
     d = lax.axis_index("dp")
@@ -75,17 +75,35 @@
         pltpu.make_async_copy(sv, lv.at[pl.ds(0, TOK)], loc.at[1]),
         pltpu.make_async_copy(bt, lv.at[pl.ds(TOK, RANK)], loc.at[2]),
     ]
+    locals_.append(pltpu.make_async_copy(a_in, a, loc.at[7]))
+    locals_.append(pltpu.make_async_copy(mag_in, mag, loc.at[8]))
     for i in range(4):
         rows = pl.ds(i * (FEAT // 4), FEAT // 4)
         locals_.append(pltpu.make_async_copy(w.at[rows], wv.at[rows], loc.at[3 + i]))
     for cp in locals_:
         cp.start()
 
+    def signal(sem, to):
+        pl.semaphore_signal(sem, inc=1, device_id=to, device_id_type=MESH)
+
+    def meet(sem, step):
+        @pl.when(z >= step)
+        def _():
+            signal(sem, dev(z_=z - step))
+
+        @pl.when(z + step < RINGS)
+        def _():
+            signal(sem, dev(z_=z + step))
+
+    def met(step):
+        return jnp.where(z >= step, 1, 0) + jnp.where(z + step < RINGS, 1, 0)
+
     barrier = pltpu.get_barrier_semaphore()
-    peers = [up, down, pair, mate, across] + ring
-    for to in peers:
-        pl.semaphore_signal(barrier, inc=1, device_id=to, device_id_type=MESH)
-    pl.semaphore_wait(barrier, len(peers))
+    near = [up, down, pair, mate, across]
+    for to in near:
+        signal(barrier, to)
+    meet(barrier, 1)
+    pl.semaphore_wait(barrier, len(near) + met(1))
 
     kcp = remote(kg, kc.at[t], ts.at[0], tr.at[0], pair)
     fwd, grad = [], []
@@ -99,11 +117,15 @@
         at = (slice(None), pl.ds(i * narrow, narrow))
         grad.append(remote(sg.at[at], gr.at[at], gs.at[i], gf.at[i], down))
 
+    meet(know.at[0], 1)
+
     raw[...] = jnp.zeros_like(raw)
     low[...] = jnp.zeros_like(low)
     sq[...] = jnp.zeros_like(sq)
     for cp in locals_:
         cp.wait()
+    pl.semaphore_wait(know.at[0], met(1))
+    meet(know.at[1], 2)
 
     @pl.loop(0, FEAT // DEPTH)
     def _(i):
@@ -117,6 +139,8 @@
         sq[...] += jnp.sum((combined * combined).reshape(DEPTH // 8, 8, COLS), axis=0)
 
     sqc = remote(sq, sqr, ts.at[1], tr.at[1], pair)
+    pl.semaphore_wait(know.at[1], met(2))
+    meet(know.at[2], 4)
 
     av = a[...]
     lows = low[pl.ds(0, TOK), :]
@@ -165,6 +189,7 @@
 
     pl.loop(0, GRAD_PIECES // 2)(stream_piece)
 
+    pl.semaphore_wait(know.at[2], met(4))
     s1c.wait_recv()
     zs[z] = s1[...] + s1r[...]
     zsc = [remote(zs.at[z], zs.at[z], zsd.at[k], zrv.at[k], to) for k, to in enumerate(ring)]
@@ -188,15 +213,10 @@
 
     pl.loop(GRAD_PIECES // 2, GRAD_PIECES)(stream_piece)
 
-    writes = []
-
     def finish_grad(i):
         grad[i].wait_recv()
         at = (slice(None), pl.ds(i * narrow, narrow))
-        st[at] = (sp[at] + gr[at].astype(F32)).astype(BF)
-        cp = pltpu.make_async_copy(st.at[at], so.at[at], outs.at[i])
-        cp.start()
-        writes.append(cp)
+        so[at] = (sp[at] + gr[at].astype(F32)).astype(BF)
 
     def take_forward(i):
         fwd[i].wait_recv()
@@ -280,8 +300,29 @@
 
     for cp in [kcp, sqc, s0c, oxc, indc, s1c, o2c, fpc, s3c, o4c, c0c] + zsc + o3c + sbc + fwd + grad:
         cp.wait_send()
-    for cp in writes:
-        cp.wait()
+
+
+def hand_over(*results):
+    count = len(results)
+
+    def copies(*refs):
+        moves = [
+            pltpu.make_async_copy(refs[i], refs[count + i], refs[-1].at[i]) for i in range(count)
+        ]
+        for cp in moves:
+            cp.start()
+        for cp in moves:
+            cp.wait()
+
+    return pl.pallas_call(
+        copies,
+        out_shape=[jax.ShapeDtypeStruct(r.shape, r.dtype) for r in results],
+        in_specs=[pl.BlockSpec(memory_space=pl.ANY)] * count,
+        out_specs=[pl.BlockSpec(memory_space=pl.ANY)] * count,
+        scratch_shapes=[pltpu.SemaphoreType.DMA((count,))],
+        compiler_params=pltpu.CompilerParams(vmem_limit_bytes=2**20),
+        name="hand_over",
+    )(*results)
 
 
 def per_device(section_out, saved_stream, section_grad, key_grad, key_weight, adapter_in, adapter_out, magnitude):
@@ -293,18 +334,19 @@
     keys, so, mg, og, ig = pl.pallas_call(
         kernel,
         out_shape=[
-            jax.ShapeDtypeStruct((HALF, COLS), BF),
-            jax.ShapeDtypeStruct((TOK, FEAT), BF),
-            jax.ShapeDtypeStruct((1, COLS), F32),
-            jax.ShapeDtypeStruct((OUTROWS, RANK), F32),
-            jax.ShapeDtypeStruct((RANK, SHARE), F32),
+            V((HALF, COLS), BF),
+            V((TOK, FEAT), BF),
+            V((1, COLS), F32),
+            V((OUTROWS, RANK), F32),
+            V((RANK, SHARE), F32),
         ],
-        in_specs=[hbm] * 6 + [vmem] * 2,
-        out_specs=[vmem, hbm, vmem, vmem, vmem],
+        in_specs=[hbm] * 8,
+        out_specs=[vmem] * 5,
         scratch_shapes=[
+            V((RANK, COLS), BF),
+            V((1, COLS), F32),
             V((FEAT, COLS), BF),
             V((TOK + RANK, FEAT), BF),
-            V((TOK, FEAT), BF),
             V((TOK, FEAT), BF),
             V((TOK, FEAT), BF),
             V((TOK, FEAT), F32),
@@ -341,8 +383,7 @@
             V((HALF, COLS), F32),
             V((HALF, COLS), F32),
             V((COLS, 8), F32),
-            dma((7,)),
-            dma((GRAD_PIECES,)),
+            dma((9,)),
             dma((GRAD_PIECES,)),
             dma((GRAD_PIECES,)),
             dma((GRAD_PIECES,)),
@@ -355,21 +396,22 @@
             dma((21,)),
             dma((3,)),
             dma((3,)),
+            pltpu.SemaphoreType.REGULAR((3,)),
         ],
         compiler_params=pltpu.CompilerParams(
-            collective_id=0, has_side_effects=True, vmem_limit_bytes=56 * 2**20
+            collective_id=0, has_side_effects=True, vmem_limit_bytes=40 * 2**20
         ),
         name="relay_tick",
     )(
-        section_out[0],
-        saved_stream[0],
-        section_grad[0],
-        key_grad[0],
-        key_weight[0],
-        adapter_in[0].T,
-        adapter_out[0],
-        magnitude,
+        *[
+            pltpu.with_memory_space_constraint(value, pltpu.HBM)
+            for value in (
+                section_out[0], saved_stream[0], section_grad[0], key_grad[0],
+                key_weight[0], adapter_in[0].T, adapter_out[0], magnitude,
+            )
+        ]
     )
+    keys, so, mg, og, ig = hand_over(keys, so, mg, og, ig)
     return (keys[None], so[None], mg, og.T[None], ig.T[None])
 
 

time: 67.6 us -> 56.6 us (0.84)
  the two profiles are of different devices: /device:TPU:2 before, /device:TPU:64 now
where the time goes in v2:
time: 56.6 us; the launch traced here: 56.1 us
  Pallas kernels  55.4 us (98%)
  between operations  0.64 us (1%)
    pallas_call x1, Pallas kernels, per_device(): pl.pallas_call(kernel, out_shape=[V((HALF, COLS), BF), V((TOK, FEAT), BF)...  54 us
    pallas_call x1, Pallas kernels, hand_over(): pl.pallas_call(copies, out_shape=[jax.ShapeDtypeStruct(r.shape, r.dtype)...  1.4 us

profile of v2, /device:TPU:64, one launch (start us, length us, event | category | flops | bytes accessed | tf_op | source)
XLA Modules:
  0.0 56.1 jit_solution(10501982348690366569)
XLA Ops:
  0.6 54.0 %relay_tick.1 = (bf16[64,512]{1,0:T(8,128)(2,1)S(1)}, bf16[128,8192]{1,0:T(8,128)(2,1)S(1)}, f32[1,512]{1,0:T(1,128)S(1)}, f32[16,64]{1,0:T(8,128)S(1)}, f32[64,256]{1,0:T(8,128)S(1)}) custom-call(bf16[128,8192]{1,0:T(8,128)(2,1)} %bitcast.18, bf16[128,8192]{1,0:T(8,128)(2,1)} %bitcast.19, bf16[128,8192]{1,0:T(8,128)(2,1)} %bitcast.20, ...), custom_call_target="tpu_custom_call" | custom-call | tf_op jit(solution)/shard_map/relay_tick/pallas_call | solution.py:334
  54.7 1.4 %hand_over.1 = (bf16[64,512]{1,0:T(8,128)(2,1)}, bf16[128,8192]{1,0:T(8,128)(2,1)}, f32[1,512]{1,0:T(1,128)}, f32[16,64]{1,0:T(8,128)}, f32[64,256]{1,0:T(8,128)}) custom-call(bf16[64,512]{1,0:T(8,128)(2,1)S(1)} %get-tuple-element.15.refs_0_, bf16[128,8192]{1,0:T(8,128)(2,1)S(1)} %get-tuple-element.16.refs_1_, f32[1,512]{1,0:T(1,128)S(1)} %get-tuple-element.17.refs_2_, ...), custom_call_target="tpu_custom_call" | custom-call | tf_op jit(solution)/shard_map/hand_over/pallas_call | solution.py:317

commit v3 on v2

v3 whole, which is shorter than its diff:
```python
import jax
import jax.numpy as jnp
from jax import lax
from jax.experimental import pallas as pl
from jax.experimental.pallas import tpu as pltpu
from jax.sharding import PartitionSpec as P

EPSILON = 1e-06
MESH = pl.DeviceIdType.MESH
BF = jnp.bfloat16
F32 = jnp.float32

PIPES = 4
REPLICAS = 32
HUB = 2
RINGS = 8
TOK = 128
HALF = 64
COLS = 512
RANK = 64
FEAT = 8192
SHARE = FEAT // REPLICAS
OUTROWS = COLS // REPLICAS
DEPTH = 512
STREAM = 1024
FWD_PIECES = (
    (False, 0, 4096),
    (False, 4096, 4096),
    (True, 0, 4096),
    (True, 4096, 2048),
    (True, 6144, 1536),
    (True, 7680, 512),
)
GRAD_PIECES = 8
GRAD_ROWS = TOK // GRAD_PIECES


def mm(left, right, left_dim, right_dim):
    return lax.dot_general(
        left, right, (((left_dim,), (right_dim,)), ((), ())), preferred_element_type=F32
    )


def halves(value):
    upper = value.astype(BF)
    lower = (value - upper.astype(F32)).astype(BF)
    return upper, lower


def mm2(wide, narrow, left_dim, right_dim):
    upper, lower = halves(wide)
    return mm(upper, narrow, left_dim, right_dim) + mm(lower, narrow, left_dim, right_dim)


def kernel(
    x, sv, sg, kg, w, bt, a_in, mag_in,
    keys, so, mg, og, ig,
    a, mag, wv, bv, lv, fw, gr, sp, kc, raw, low, sqs, ksb, lgv, fac, flo,
    ox, oxr, o2, o2r, o3, o3r, o4, o4r,
    s0, s0r, s1, s1r, zs, s3, s3r,
    im, io, ra, sb, rb, c0, rc, fp, fpr, cv,
    loc, fs, fr, gs, gf, ts, tr, cs, cr, zsd, zrv, hs, hr, qs, qr, know,
):
    p = lax.axis_index("pipe")
    d = lax.axis_index("dp")
    t = lax.axis_index("tensor")
    z, h, c = d // 4, (d // 2) % 2, d % 2

    def dev(p_=p, z_=z, h_=h, c_=c, t_=t):
        return {"pipe": p_, "dp": (z_ * 2 + h_) * 2 + c_, "tensor": t_}

    up, down = dev(p_=(p + 1) % PIPES), dev(p_=(p + PIPES - 1) % PIPES)
    pair, mate, across = dev(t_=1 - t), dev(c_=1 - c), dev(h_=1 - h)
    both_other = dev(t_=1 - t, c_=1 - c)
    ring = [dev(z_=(z + k) % RINGS) for k in range(1, RINGS)]

    def remote(src, dst, ssem, rsem, to):
        cp = pltpu.make_async_remote_copy(
            src_ref=src, dst_ref=dst, send_sem=ssem, recv_sem=rsem, device_id=to, device_id_type=MESH
        )
        cp.start()
        return cp

    mine = pl.ds(pl.multiple_of(c * (FEAT // 2), FEAT // 2), FEAT // 2)
    others = pl.ds(pl.multiple_of((1 - c) * (FEAT // 2), FEAT // 2), FEAT // 2)
    first = [
        pltpu.make_async_copy(a_in, a, loc.at[0]),
        pltpu.make_async_copy(mag_in, mag, loc.at[1]),
        pltpu.make_async_copy(bt, bv, loc.at[2]),
        pltpu.make_async_copy(w.at[mine], wv.at[mine], loc.at[3]),
    ]
    second = [
        pltpu.make_async_copy(kg, kc.at[t], loc.at[4]),
        pltpu.make_async_copy(sv, lv, loc.at[5]),
        pltpu.make_async_copy(w.at[others], wv.at[others], loc.at[6]),
    ]
    for cp in first + second:
        cp.start()

    def signal(sem, to):
        pl.semaphore_signal(sem, inc=1, device_id=to, device_id_type=MESH)

    def meet(sem, step):
        @pl.when(z >= step)
        def _():
            signal(sem, dev(z_=z - step))

        @pl.when(z + step < RINGS)
        def _():
            signal(sem, dev(z_=z + step))

    def met(step):
        return jnp.where(z >= step, 1, 0) + jnp.where(z + step < RINGS, 1, 0)

    barrier = pltpu.get_barrier_semaphore()
    near = [up, down, pair, mate, both_other]
    for to in near:
        signal(barrier, to)

    @pl.when(p == HUB)
    def _():
        signal(barrier, across)
        meet(barrier, 1)

    pl.semaphore_wait(barrier, len(near) + jnp.where(p == HUB, 1 + met(1), 0))

    fwd, grad = [], []
    for i in range(len(FWD_PIECES)):
        own, start, width = FWD_PIECES[i]
        rows = pl.ds(pl.multiple_of((t if own else 1 - t) * HALF, HALF), HALF)
        at = (rows, pl.ds(start, width))
        fwd.append(remote(x.at[at], fw.at[at], fs.at[i], fr.at[i], up))
    for i in range(GRAD_PIECES):
        at = pl.ds(i * GRAD_ROWS, GRAD_ROWS)
        grad.append(remote(sg.at[at], gr.at[at], gs.at[i], gf.at[i], down))
    kcp = remote(kg, kc.at[t], ts.at[0], tr.at[0], pair)

    @pl.when(p == HUB - 1)
    def _():
        signal(know.at[0], up)

    @pl.when(p == HUB)
    def _():
        pl.semaphore_wait(know.at[0], 1)
        signal(know.at[1], across)
        meet(know.at[1], 1)

    here = t * 2 + c
    sqs[here] = jnp.zeros((8, COLS), F32)
    for cp in first:
        cp.wait()
    av = a[...]

    @pl.when(p == HUB)
    def _():
        pl.semaphore_wait(know.at[1], 1 + met(1))
        meet(know.at[2], 2)

    @pl.loop(0, FEAT // 2 // DEPTH)
    def _(i):
        part = pl.ds(pl.multiple_of(c * (FEAT // 2) + i * DEPTH, DEPTH), DEPTH)
        combined = wv[part, :].astype(F32) + mm(bv[:, part], a[...], 0, 0)
        sqs[here] += jnp.sum((combined * combined).reshape(DEPTH // 8, 8, COLS), axis=0)

    sqc = [
        remote(sqs.at[here], sqs.at[here], qs.at[k], qr.at[k], to)
        for k, to in enumerate([pair, mate, both_other])
    ]

    @pl.when(p == HUB)
    def _():
        pl.semaphore_wait(know.at[2], met(2))
        meet(know.at[3], 4)

    raw[...] = jnp.zeros_like(raw)
    low[...] = jnp.zeros_like(low)
    for cp in second:
        cp.wait()

    @pl.loop(0, FEAT // DEPTH)
    def _(i):
        part = pl.ds(pl.multiple_of(i * DEPTH, DEPTH), DEPTH)
        left = lv[:, part]
        raw[...] += mm(left, wv[part, :], 1, 0)
        low[...] += mm(left, bv[:, part], 1, 1)

    kcp.wait_recv()
    cot = kc[...].reshape(TOK, COLS)
    for cp in sqc:
        cp.wait_recv()
    norm = jnp.sqrt(
        jnp.sum((sqs[0] + sqs[1]) + (sqs[2] + sqs[3]), axis=0, keepdims=True) + EPSILON
    )
    scale = mag[...] / norm
    shi, slo = halves(cot.astype(F32) * scale)
    ksb[...] = shi
    low_grad = mm(shi, av, 1, 1) + mm(slo, av, 1, 1)
    lgv[...] = low_grad.astype(BF)
    turned_grad = low_grad.T.astype(BF)

    def token_sum(i, core):
        part = pl.ds(pl.multiple_of((i * 2 + core) * SHARE, SHARE), SHARE)
        return mm(turned_grad, lv[:, part], 1, 0)

    @pl.loop(0, REPLICAS // 2)
    def _(i):
        im[i] = token_sum(i, 1 - c)

    imc = remote(im, ra, cs.at[0], cr.at[0], mate)

    @pl.when(p == HUB)
    def _():
        pl.semaphore_wait(know.at[3], met(4))
        signal(know.at[4], up)
        signal(know.at[4], down)

    lhi, llo = halves(low[...])
    raw_saved = raw[...] + mm(lhi, av, 1, 0) + mm(llo, av, 1, 0)
    s0[...] = jnp.sum((cot.astype(F32) * raw_saved).reshape(TOK // 8, 8, COLS), axis=0)
    s0c = remote(s0, s0r, ts.at[1], tr.at[1], pair)
    part = pl.ds(pl.multiple_of(d * SHARE, SHARE), SHARE)
    b_share = bv[:, part]
    cross = mm(b_share, wv[part, :], 1, 0) + mm2(mm(b_share, b_share, 1, 1), av, 1, 0)
    ox[:, pl.ds(0, RANK)] = mm(cot, lhi, 0, 0) + mm(cot, llo, 0, 0)
    ox[:, pl.ds(RANK, RANK)] = cross.T
    oxc = remote(ox, oxr, ts.at[2], tr.at[2], pair)

    @pl.when(p == HUB - 1)
    def _():
        pl.semaphore_wait(know.at[4], 1)
        signal(know.at[4], down)

    @pl.loop(0, REPLICAS // 2)
    def _(i):
        io[i] = token_sum(i, c)

    s0c.wait_recv()
    s1[...] = s0[...] + s0r[...]
    s1c = remote(s1, s1r, cs.at[1], cr.at[1], mate)

    imc.wait_recv()

    @pl.when((p == HUB + 1) | (p == HUB - 2))
    def _():
        pl.semaphore_wait(know.at[4], 1)

    @pl.loop(0, RINGS)
    def _(i):
        for k in range(2):
            sb[i, k] = (io[i * 2 + k] + ra[i * 2 + k]).astype(BF)

    sbc = [
        remote(sb.at[(z + k + 1) % RINGS], rb.at[z], zsd.at[14 + k], zrv.at[14 + k], to)
        for k, to in enumerate(ring)
    ]

    oxc.wait_recv()
    sums = (ox[...] + oxr[...]).reshape(REPLICAS // 2, 2, OUTROWS, 2 * RANK)
    o2[0] = sums[:, 0]
    o2[1] = sums[:, 1]
    o2c = remote(o2.at[1 - c], o2r, cs.at[2], cr.at[2], mate)

    def stream_piece(i):
        part = pl.ds(pl.multiple_of(i * STREAM, STREAM), STREAM)
        sp[:, part] = mm(ksb[...], wv[part, :], 1, 1) + mm(lgv[...], bv[:, part], 1, 0)

    pl.loop(0, FEAT // STREAM // 2)(stream_piece)

    s1c.wait_recv()
    zs[z] = s1[...] + s1r[...]
    zsc = [remote(zs.at[z], zs.at[z], zsd.at[k], zrv.at[k], to) for k, to in enumerate(ring)]
    o2c.wait_recv()
    o3[...] = (o2[c] + o2r[...]).reshape(RINGS, 2, OUTROWS, 2 * RANK)
    o3c = [
        remote(o3.at[(z + k + 1) % RINGS], o3r.at[z], zsd.at[7 + k], zrv.at[7 + k], to)
        for k, to in enumerate(ring)
    ]

    pl.loop(FEAT // STREAM // 2, FEAT // STREAM)(stream_piece)

    def finish_grad(i):
        grad[i].wait_recv()
        at = pl.ds(i * GRAD_ROWS, GRAD_ROWS)
        so[at] = (sp[at] + gr[at].astype(F32)).astype(BF)

    def take_forward(i):
        fwd[i].wait_recv()
        own, start, width = FWD_PIECES[i]
        rows = pl.ds(pl.multiple_of((t if own else 1 - t) * HALF, HALF), HALF)
        if start == 0:
            fac[...] = jnp.zeros_like(fac)
            flo[...] = jnp.zeros_like(flo)

        @pl.loop(0, width // DEPTH)
        def _(k):
            part = pl.ds(pl.multiple_of(start + k * DEPTH, DEPTH), DEPTH)
            rowsv = fw[rows, part]
            fac[...] += mm(rowsv, wv[part, :], 1, 0)
            flo[...] += mm(rowsv, bv[:, part], 1, 1)

    def partial_keys():
        return fac[...] + mm2(flo[...], a[...], 1, 0)

    take_forward(0)
    finish_grad(0)
    take_forward(1)
    finish_grad(1)
    finish_grad(2)
    finish_grad(3)
    fp[...] = partial_keys()
    fpc = remote(fp, fpr, ts.at[3], tr.at[3], pair)

    for cp in zsc:
        cp.wait_recv()
    total = zs[0]
    for k in range(1, RINGS):
        total = total + zs[k]
    s3[...] = total
    s3c = remote(s3, s3r, hs.at[0], hr.at[0], across)
    for cp in o3c:
        cp.wait_recv()
    total = o3[z]
    for k in range(1, RINGS):
        total = total + o3r[(z + k) % RINGS]
    o4[...] = total
    o4c = remote(o4.at[1 - h], o4r, hs.at[1], hr.at[1], across)

    for cp in sbc:
        cp.wait_recv()
    for k in range(2):
        total = io[z * 2 + k] + ra[z * 2 + k]
        for n in range(1, RINGS):
            total = total + rb[(z + n) % RINGS, k].astype(F32)
        c0[k] = total
    c0c = remote(c0.at[1 - h], rc, hs.at[2], hr.at[2], across)

    take_forward(2)
    finish_grad(4)
    s3c.wait_recv()
    scale_grad = jnp.sum(s3[...] + s3r[...], axis=0, keepdims=True)
    factor = -scale_grad * mag[...] / (norm * norm * norm)
    mg[...] = scale_grad / norm / REPLICAS
    columns = jnp.concatenate([scale, factor, jnp.zeros((6, COLS), F32)], axis=0)
    cv[...] = columns.T
    o4c.wait_recv()
    lines = pl.ds(pl.multiple_of(d * OUTROWS, OUTROWS), OUTROWS)
    whole = o4[h] + o4r[...]
    og[...] = (
        whole[:, :RANK] * cv[lines, pl.ds(0, 1)] + whole[:, RANK:] * cv[lines, pl.ds(1, 1)]
    ) / REPLICAS
    turned = a[...].astype(F32) * factor
    thi, tlo = halves(turned)
    part = pl.ds(pl.multiple_of(d * SHARE, SHARE), SHARE)
    wsh = wv[part, :]
    small = mm(thi, a[...], 1, 1) + mm(tlo, a[...], 1, 1)
    term = mm(thi, wsh, 1, 1) + mm(tlo, wsh, 1, 1) + mm2(small, bv[:, part], 1, 0)

    finish_grad(5)
    take_forward(3)
    c0c.wait_recv()
    ig[...] = (c0[h] + rc[...] + term) / REPLICAS
    fpc.wait_recv()
    finish_grad(6)
    take_forward(4)
    take_forward(5)
    keys[...] = ((partial_keys() + fpr[...]) * scale).astype(BF)
    finish_grad(7)

    for cp in [kcp, s0c, oxc, imc, s1c, o2c, fpc, s3c, o4c, c0c] + sqc + zsc + o3c + sbc + fwd + grad:
        cp.wait_send()


def hand_over(*results):
    count = len(results)
    places = []
    for i, value in enumerate(results):
        rows = value.shape[0]
        cuts = 8 if rows == TOK else 1
        places += [(i, pl.ds(k * (rows // cuts), rows // cuts)) for k in range(cuts)]

    def copies(*refs):
        moves = [
            pltpu.make_async_copy(refs[i].at[at], refs[count + i].at[at], refs[-1].at[k])
            for k, (i, at) in enumerate(places)
        ]
        for cp in moves:
            cp.start()
        for cp in moves:
            cp.wait()

    return pl.pallas_call(
        copies,
        out_shape=[jax.ShapeDtypeStruct(r.shape, r.dtype) for r in results],
        in_specs=[pl.BlockSpec(memory_space=pl.ANY)] * count,
        out_specs=[pl.BlockSpec(memory_space=pl.ANY)] * count,
        scratch_shapes=[pltpu.SemaphoreType.DMA((len(places),))],
        compiler_params=pltpu.CompilerParams(vmem_limit_bytes=2**20),
        name="hand_over",
    )(*results)


def per_device(section_out, saved_stream, section_grad, key_grad, key_weight, adapter_in, adapter_out, magnitude):
    vmem = pl.BlockSpec(memory_space=pltpu.VMEM)
    hbm = pl.BlockSpec(memory_space=pl.ANY)
    dma = pltpu.SemaphoreType.DMA
    V = pltpu.VMEM
    half = REPLICAS // 2
    keys, so, mg, og, ig = pl.pallas_call(
        kernel,
        out_shape=[
            V((HALF, COLS), BF),
            V((TOK, FEAT), BF),
            V((1, COLS), F32),
            V((OUTROWS, RANK), F32),
            V((RANK, SHARE), F32),
        ],
        in_specs=[hbm] * 8,
        out_specs=[vmem] * 5,
        scratch_shapes=[
            V((RANK, COLS), BF),
            V((1, COLS), F32),
            V((FEAT, COLS), BF),
            V((RANK, FEAT), BF),
            V((TOK, FEAT), BF),
            V((TOK, FEAT), BF),
            V((TOK, FEAT), BF),
            V((TOK, FEAT), F32),
            V((2, HALF, COLS), BF),
            V((TOK, COLS), F32),
            V((TOK, RANK), F32),
            V((4, 8, COLS), F32),
            V((TOK, COLS), BF),
            V((TOK, RANK), BF),
            V((HALF, COLS), F32),
            V((HALF, RANK), F32),
            V((COLS, 2 * RANK), F32),
            V((COLS, 2 * RANK), F32),
            V((2, half, OUTROWS, 2 * RANK), F32),
            V((half, OUTROWS, 2 * RANK), F32),
            V((RINGS, 2, OUTROWS, 2 * RANK), F32),
            V((RINGS, 2, OUTROWS, 2 * RANK), F32),
            V((2, OUTROWS, 2 * RANK), F32),
            V((OUTROWS, 2 * RANK), F32),
            V((8, COLS), F32),
            V((8, COLS), F32),
            V((8, COLS), F32),
            V((8, COLS), F32),
            V((RINGS, 8, COLS), F32),
            V((8, COLS), F32),
            V((8, COLS), F32),
            V((half, RANK, SHARE), F32),
            V((half, RANK, SHARE), F32),
            V((half, RANK, SHARE), F32),
            V((RINGS, 2, RANK, SHARE), BF),
            V((RINGS, 2, RANK, SHARE), BF),
            V((2, RANK, SHARE), F32),
            V((RANK, SHARE), F32),
            V((HALF, COLS), F32),
            V((HALF, COLS), F32),
            V((COLS, 8), F32),
            dma((7,)),
            dma((len(FWD_PIECES),)),
            dma((len(FWD_PIECES),)),
            dma((GRAD_PIECES,)),
            dma((GRAD_PIECES,)),
            dma((4,)),
            dma((4,)),
            dma((3,)),
            dma((3,)),
            dma((21,)),
            dma((21,)),
            dma((3,)),
            dma((3,)),
            dma((3,)),
            dma((3,)),
            pltpu.SemaphoreType.REGULAR((5,)),
        ],
        compiler_params=pltpu.CompilerParams(
            collective_id=0, has_side_effects=True, vmem_limit_bytes=40 * 2**20
        ),
        name="relay_tick",
    )(
        *[
            pltpu.with_memory_space_constraint(value, pltpu.HBM)
            for value in (
                section_out[0], saved_stream[0], section_grad[0], key_grad[0],
                key_weight[0], adapter_in[0].T, adapter_out[0], magnitude,
            )
        ]
    )
    keys, so, mg, og, ig = hand_over(keys, so, mg, og, ig)
    return (keys[None], so[None], mg, og.T[None], ig.T[None])


def solution(mesh):
    placed = (
        P("pipe", "dp", "tensor"),
        P("pipe", "dp", "tensor"),
        P("pipe", "dp", "tensor"),
        P("pipe", ("dp", "tensor"), None),
        P("pipe", "tensor", None),
        P("pipe", "tensor", None),
        P("pipe", None, None),
        P("pipe", None),
    )
    return jax.shard_map(
        per_device,
        mesh=mesh,
        in_specs=placed,
        out_specs=(
            P("pipe", ("dp", "tensor"), None),
            P("pipe", "dp", "tensor"),
            P("pipe", None),
            P("pipe", None, "dp"),
            P("pipe", ("tensor", "dp"), None),
        ),
        check_vma=False,
    )
```

time: 56.6 us -> 54.7 us (0.966)
  Pallas kernels: 55.4 us -> 53.8 us
    pallas_call x1, Pallas kernels: 54 us -> 52.4 us  [per_device(): pl.pallas_call(kernel, out_shape=[V((HALF, COLS), BF), V((TOK, FEAT), BF)...]
where the time goes in v3:
time: 54.7 us; the launch traced here: 54.5 us
  Pallas kernels  53.8 us (98%)
  between operations  0.64 us (1%)
    pallas_call x1, Pallas kernels, per_device(): pl.pallas_call(kernel, out_shape=[V((HALF, COLS), BF), V((TOK, FEAT), BF)...  52.4 us
    pallas_call x1, Pallas kernels, hand_over(): pl.pallas_call(copies, out_shape=[jax.ShapeDtypeStruct(r.shape, r.dtype)...  1.46 us

profile of v3, /device:TPU:64, one launch (start us, length us, event | category | flops | bytes accessed | tf_op | source)
XLA Modules:
  0.0 54.5 jit_solution(1218160064742754488)
XLA Ops:
  0.6 52.4 %relay_tick.1 = (bf16[64,512]{1,0:T(8,128)(2,1)S(1)}, bf16[128,8192]{1,0:T(8,128)(2,1)S(1)}, f32[1,512]{1,0:T(1,128)S(1)}, f32[16,64]{1,0:T(8,128)S(1)}, f32[64,256]{1,0:T(8,128)S(1)}) custom-call(bf16[128,8192]{1,0:T(8,128)(2,1)} %bitcast.18, bf16[128,8192]{1,0:T(8,128)(2,1)} %bitcast.19, bf16[128,8192]{1,0:T(8,128)(2,1)} %bitcast.20, ...), custom_call_target="tpu_custom_call" | custom-call | tf_op jit(solution)/shard_map/relay_tick/pallas_call | solution.py:408
  53.0 1.5 %hand_over.1 = (bf16[64,512]{1,0:T(8,128)(2,1)}, bf16[128,8192]{1,0:T(8,128)(2,1)}, f32[1,512]{1,0:T(1,128)}, f32[16,64]{1,0:T(8,128)}, f32[64,256]{1,0:T(8,128)}) custom-call(bf16[64,512]{1,0:T(8,128)(2,1)S(1)} %get-tuple-element.15.refs_0_, bf16[128,8192]{1,0:T(8,128)(2,1)S(1)} %get-tuple-element.16.refs_1_, f32[1,512]{1,0:T(1,128)S(1)} %get-tuple-element.17.refs_2_, ...), custom_call_target="tpu_custom_call" | custom-call | tf_op jit(solution)/shard_map/hand_over/pallas_call | solution.py:391

commit v4 on v3

--- a/solution.py
+++ b/solution.py
@@ -81,6 +81,34 @@
         cp.start()
         return cp
 
+    def signal(sem, to):
+        pl.semaphore_signal(sem, inc=1, device_id=to, device_id_type=MESH)
+
+    def meet(sem, step):
+        @pl.when(z >= step)
+        def _():
+            signal(sem, dev(z_=z - step))
+
+        @pl.when(z + step < RINGS)
+        def _():
+            signal(sem, dev(z_=z + step))
+
+    def met(step):
+        return jnp.where(z >= step, 1, 0) + jnp.where(z + step < RINGS, 1, 0)
+
+    barrier = pltpu.get_barrier_semaphore()
+    near = [up, down, mate]
+    hub, hub_mate = (p == HUB) & (c == 0), (p == HUB) & (c == 1)
+    below, ends = p == HUB - 1, (p == HUB + 1) | (p == HUB - 2)
+    for to in near:
+        signal(barrier, to)
+
+    @pl.when(hub)
+    def _():
+        signal(barrier, pair)
+        signal(barrier, across)
+        meet(barrier, 1)
+
     mine = pl.ds(pl.multiple_of(c * (FEAT // 2), FEAT // 2), FEAT // 2)
     others = pl.ds(pl.multiple_of((1 - c) * (FEAT // 2), FEAT // 2), FEAT // 2)
     first = [
@@ -97,53 +125,36 @@
     for cp in first + second:
         cp.start()
 
-    def signal(sem, to):
-        pl.semaphore_signal(sem, inc=1, device_id=to, device_id_type=MESH)
-
-    def meet(sem, step):
-        @pl.when(z >= step)
-        def _():
-            signal(sem, dev(z_=z - step))
-
-        @pl.when(z + step < RINGS)
-        def _():
-            signal(sem, dev(z_=z + step))
-
-    def met(step):
-        return jnp.where(z >= step, 1, 0) + jnp.where(z + step < RINGS, 1, 0)
-
-    barrier = pltpu.get_barrier_semaphore()
-    near = [up, down, pair, mate, both_other]
-    for to in near:
-        signal(barrier, to)
-
-    @pl.when(p == HUB)
-    def _():
-        signal(barrier, across)
-        meet(barrier, 1)
-
-    pl.semaphore_wait(barrier, len(near) + jnp.where(p == HUB, 1 + met(1), 0))
+    pl.semaphore_wait(barrier, len(near) + jnp.where(hub, 2 + met(1), 0))
 
     fwd, grad = [], []
-    for i in range(len(FWD_PIECES)):
-        own, start, width = FWD_PIECES[i]
-        rows = pl.ds(pl.multiple_of((t if own else 1 - t) * HALF, HALF), HALF)
-        at = (rows, pl.ds(start, width))
-        fwd.append(remote(x.at[at], fw.at[at], fs.at[i], fr.at[i], up))
     for i in range(GRAD_PIECES):
+        if i < len(FWD_PIECES):
+            own, start, width = FWD_PIECES[i]
+            rows = pl.ds(pl.multiple_of((t if own else 1 - t) * HALF, HALF), HALF)
+            at = (rows, pl.ds(start, width))
+            fwd.append(remote(x.at[at], fw.at[at], fs.at[i], fr.at[i], up))
         at = pl.ds(i * GRAD_ROWS, GRAD_ROWS)
         grad.append(remote(sg.at[at], gr.at[at], gs.at[i], gf.at[i], down))
-    kcp = remote(kg, kc.at[t], ts.at[0], tr.at[0], pair)
-
-    @pl.when(p == HUB - 1)
+
+    @pl.when(below)
     def _():
         signal(know.at[0], up)
 
-    @pl.when(p == HUB)
+    @pl.when(hub_mate)
     def _():
         pl.semaphore_wait(know.at[0], 1)
+        signal(know.at[0], mate)
+
+    @pl.when(hub)
+    def _():
+        pl.semaphore_wait(know.at[0], 2)
+        signal(know.at[5], pair)
         signal(know.at[1], across)
         meet(know.at[1], 1)
+        pl.semaphore_wait(know.at[5], 1)
+        for to in near:
+            signal(know.at[6], to)
 
     here = t * 2 + c
     sqs[here] = jnp.zeros((8, COLS), F32)
@@ -151,7 +162,13 @@
         cp.wait()
     av = a[...]
 
-    @pl.when(p == HUB)
+    @pl.when(hub_mate)
+    def _():
+        pl.semaphore_wait(know.at[6], 1)
+        signal(know.at[6], up)
+        signal(know.at[6], down)
+
+    @pl.when(hub)
     def _():
         pl.semaphore_wait(know.at[1], 1 + met(1))
         meet(know.at[2], 2)
@@ -162,27 +179,40 @@
         combined = wv[part, :].astype(F32) + mm(bv[:, part], a[...], 0, 0)
         sqs[here] += jnp.sum((combined * combined).reshape(DEPTH // 8, 8, COLS), axis=0)
 
+    @pl.when(below)
+    def _():
+        pl.semaphore_wait(know.at[6], 1)
+        signal(know.at[6], down)
+
+    @pl.when(hub)
+    def _():
+        pl.semaphore_wait(know.at[2], met(2))
+        meet(know.at[3], 4)
+
+    raw[...] = jnp.zeros_like(raw)
+    low[...] = jnp.zeros_like(low)
+    for cp in second:
+        cp.wait()
+
+    def saved_piece(i):
+        part = pl.ds(pl.multiple_of(i * DEPTH, DEPTH), DEPTH)
+        left = lv[:, part]
+        raw[...] += mm(left, wv[part, :], 1, 0)
+        low[...] += mm(left, bv[:, part], 1, 1)
+
+    pl.loop(0, FEAT // DEPTH // 2)(saved_piece)
+
+    @pl.when(ends)
+    def _():
+        pl.semaphore_wait(know.at[6], 1)
+
+    kcp = remote(kg, kc.at[t], ts.at[0], tr.at[0], pair)
     sqc = [
         remote(sqs.at[here], sqs.at[here], qs.at[k], qr.at[k], to)
         for k, to in enumerate([pair, mate, both_other])
     ]
 
-    @pl.when(p == HUB)
-    def _():
-        pl.semaphore_wait(know.at[2], met(2))
-        meet(know.at[3], 4)
-
-    raw[...] = jnp.zeros_like(raw)
-    low[...] = jnp.zeros_like(low)
-    for cp in second:
-        cp.wait()
-
-    @pl.loop(0, FEAT // DEPTH)
-    def _(i):
-        part = pl.ds(pl.multiple_of(i * DEPTH, DEPTH), DEPTH)
-        left = lv[:, part]
-        raw[...] += mm(left, wv[part, :], 1, 0)
-        low[...] += mm(left, bv[:, part], 1, 1)
+    pl.loop(FEAT // DEPTH // 2, FEAT // DEPTH)(saved_piece)
 
     kcp.wait_recv()
     cot = kc[...].reshape(TOK, COLS)
@@ -208,11 +238,11 @@
 
     imc = remote(im, ra, cs.at[0], cr.at[0], mate)
 
-    @pl.when(p == HUB)
+    @pl.when(hub)
     def _():
         pl.semaphore_wait(know.at[3], met(4))
-        signal(know.at[4], up)
-        signal(know.at[4], down)
+        for to in near:
+            signal(know.at[4], to)
 
     lhi, llo = halves(low[...])
     raw_saved = raw[...] + mm(lhi, av, 1, 0) + mm(llo, av, 1, 0)
@@ -225,22 +255,28 @@
     ox[:, pl.ds(RANK, RANK)] = cross.T
     oxc = remote(ox, oxr, ts.at[2], tr.at[2], pair)
 
-    @pl.when(p == HUB - 1)
+    @pl.when(hub_mate)
     def _():
         pl.semaphore_wait(know.at[4], 1)
+        signal(know.at[4], up)
         signal(know.at[4], down)
 
     @pl.loop(0, REPLICAS // 2)
     def _(i):
         io[i] = token_sum(i, c)
 
+    @pl.when(below)
+    def _():
+        pl.semaphore_wait(know.at[4], 1)
+        signal(know.at[4], down)
+
     s0c.wait_recv()
     s1[...] = s0[...] + s0r[...]
     s1c = remote(s1, s1r, cs.at[1], cr.at[1], mate)
 
     imc.wait_recv()
 
-    @pl.when((p == HUB + 1) | (p == HUB - 2))
+    @pl.when(ends)
     def _():
         pl.semaphore_wait(know.at[4], 1)
 
@@ -375,7 +411,7 @@
     places = []
     for i, value in enumerate(results):
         rows = value.shape[0]
-        cuts = 8 if rows == TOK else 1
+        cuts = 2 if rows == TOK else 1
         places += [(i, pl.ds(k * (rows // cuts), rows // cuts)) for k in range(cuts)]
 
     def copies(*refs):
@@ -473,7 +509,7 @@
             dma((3,)),
             dma((3,)),
             dma((3,)),
-            pltpu.SemaphoreType.REGULAR((5,)),
+            pltpu.SemaphoreType.REGULAR((7,)),
         ],
         compiler_params=pltpu.CompilerParams(
             collective_id=0, has_side_effects=True, vmem_limit_bytes=40 * 2**20

time: 54.7 us -> 53.4 us (0.976)
  Pallas kernels: 53.8 us -> 52.7 us
    pallas_call x1, Pallas kernels: 52.4 us -> 51.3 us  [per_device(): pl.pallas_call(kernel, out_shape=[V((HALF, COLS), BF), V((TOK, FEAT), BF)...]
where the time goes in v4:
time: 53.4 us; the launch traced here: 53.3 us
  Pallas kernels  52.7 us (99%)
  between operations  0.64 us (1%)
    pallas_call x1, Pallas kernels, per_device(): pl.pallas_call(kernel, out_shape=[V((HALF, COLS), BF), V((TOK, FEAT), BF)...  51.3 us
    pallas_call x1, Pallas kernels, hand_over(): pl.pallas_call(copies, out_shape=[jax.ShapeDtypeStruct(r.shape, r.dtype)...  1.4 us

profile of v4, /device:TPU:64, one launch (start us, length us, event | category | flops | bytes accessed | tf_op | source)
XLA Modules:
  0.0 53.3 jit_solution(1828480396447996844)
XLA Ops:
  0.6 51.3 %relay_tick.1 = (bf16[64,512]{1,0:T(8,128)(2,1)S(1)}, bf16[128,8192]{1,0:T(8,128)(2,1)S(1)}, f32[1,512]{1,0:T(1,128)S(1)}, f32[16,64]{1,0:T(8,128)S(1)}, f32[64,256]{1,0:T(8,128)S(1)}) custom-call(bf16[128,8192]{1,0:T(8,128)(2,1)} %bitcast.18, bf16[128,8192]{1,0:T(8,128)(2,1)} %bitcast.19, bf16[128,8192]{1,0:T(8,128)(2,1)} %bitcast.20, ...), custom_call_target="tpu_custom_call" | custom-call | tf_op jit(solution)/shard_map/relay_tick/pallas_call | solution.py:444
  51.9 1.4 %hand_over.1 = (bf16[64,512]{1,0:T(8,128)(2,1)}, bf16[128,8192]{1,0:T(8,128)(2,1)}, f32[1,512]{1,0:T(1,128)}, f32[16,64]{1,0:T(8,128)}, f32[64,256]{1,0:T(8,128)}) custom-call(bf16[64,512]{1,0:T(8,128)(2,1)S(1)} %get-tuple-element.15.refs_0_, bf16[128,8192]{1,0:T(8,128)(2,1)S(1)} %get-tuple-element.16.refs_1_, f32[1,512]{1,0:T(1,128)S(1)} %get-tuple-element.17.refs_2_, ...), custom_call_target="tpu_custom_call" | custom-call | tf_op jit(solution)/shard_map/hand_over/pallas_call | solution.py:427

commit v5 on v4

--- a/solution.py
+++ b/solution.py
@@ -21,15 +21,15 @@
 FEAT = 8192
 SHARE = FEAT // REPLICAS
 OUTROWS = COLS // REPLICAS
-DEPTH = 512
-STREAM = 1024
+DEPTH = 1024
+STREAM = 2048
 FWD_PIECES = (
     (False, 0, 4096),
     (False, 4096, 4096),
     (True, 0, 4096),
     (True, 4096, 2048),
-    (True, 6144, 1536),
-    (True, 7680, 512),
+    (True, 6144, 1024),
+    (True, 7168, 1024),
 )
 GRAD_PIECES = 8
 GRAD_ROWS = TOK // GRAD_PIECES
@@ -327,9 +327,11 @@
             fac[...] = jnp.zeros_like(fac)
             flo[...] = jnp.zeros_like(flo)
 
-        @pl.loop(0, width // DEPTH)
+        depth = min(width, DEPTH)
+
+        @pl.loop(0, width // depth)
         def _(k):
-            part = pl.ds(pl.multiple_of(start + k * DEPTH, DEPTH), DEPTH)
+            part = pl.ds(pl.multiple_of(start + k * depth, depth), depth)
             rowsv = fw[rows, part]
             fac[...] += mm(rowsv, wv[part, :], 1, 0)
             flo[...] += mm(rowsv, bv[:, part], 1, 1)
@@ -398,11 +400,13 @@
     fpc.wait_recv()
     finish_grad(6)
     take_forward(4)
+    for cp in [kcp, s0c, oxc, imc, s1c, o2c, fpc, s3c, o4c, c0c] + sqc + zsc + o3c + sbc + fwd[:4] + grad[:6]:
+        cp.wait_send()
     take_forward(5)
     keys[...] = ((partial_keys() + fpr[...]) * scale).astype(BF)
     finish_grad(7)
 
-    for cp in [kcp, s0c, oxc, imc, s1c, o2c, fpc, s3c, o4c, c0c] + sqc + zsc + o3c + sbc + fwd + grad:
+    for cp in fwd[4:] + grad[6:]:
         cp.wait_send()
 
 
@@ -413,6 +417,7 @@
         rows = value.shape[0]
         cuts = 2 if rows == TOK else 1
         places += [(i, pl.ds(k * (rows // cuts), rows // cuts)) for k in range(cuts)]
+    places.sort(key=lambda place: -results[place[0]].size)
 
     def copies(*refs):
         moves = [

time: 53.4 us -> 53.4 us (level)
  no operation moved by 1% of the time
where the time goes in v5:
time: 53.4 us; the launch traced here: 53.3 us
  Pallas kernels  52.7 us (99%)
  between operations  0.64 us (1%)
    pallas_call x1, Pallas kernels, per_device(): pl.pallas_call(kernel, out_shape=[V((HALF, COLS), BF), V((TOK, FEAT), BF)...  51.3 us
    pallas_call x1, Pallas kernels, hand_over(): pl.pallas_call(copies, out_shape=[jax.ShapeDtypeStruct(r.shape, r.dtype)...  1.4 us

profile of v5, /device:TPU:64, one launch (start us, length us, event | category | flops | bytes accessed | tf_op | source)
XLA Modules:
  0.0 53.3 jit_solution(3211041418114207383)
XLA Ops:
  0.6 51.3 %relay_tick.1 = (bf16[64,512]{1,0:T(8,128)(2,1)S(1)}, bf16[128,8192]{1,0:T(8,128)(2,1)S(1)}, f32[1,512]{1,0:T(1,128)S(1)}, f32[16,64]{1,0:T(8,128)S(1)}, f32[64,256]{1,0:T(8,128)S(1)}) custom-call(bf16[128,8192]{1,0:T(8,128)(2,1)} %bitcast.18, bf16[128,8192]{1,0:T(8,128)(2,1)} %bitcast.19, bf16[128,8192]{1,0:T(8,128)(2,1)} %bitcast.20, ...), custom_call_target="tpu_custom_call" | custom-call | tf_op jit(solution)/shard_map/relay_tick/pallas_call | solution.py:449
  51.9 1.4 %hand_over.1 = (bf16[64,512]{1,0:T(8,128)(2,1)}, bf16[128,8192]{1,0:T(8,128)(2,1)}, f32[1,512]{1,0:T(1,128)}, f32[16,64]{1,0:T(8,128)}, f32[64,256]{1,0:T(8,128)}) custom-call(bf16[64,512]{1,0:T(8,128)(2,1)S(1)} %get-tuple-element.15.refs_0_, bf16[128,8192]{1,0:T(8,128)(2,1)S(1)} %get-tuple-element.16.refs_1_, f32[1,512]{1,0:T(1,128)S(1)} %get-tuple-element.17.refs_2_, ...), custom_call_target="tpu_custom_call" | custom-call | tf_op jit(solution)/shard_map/hand_over/pallas_call | solution.py:432

commit v6 on v5

--- a/solution.py
+++ b/solution.py
@@ -27,9 +27,9 @@
     (False, 0, 4096),
     (False, 4096, 4096),
     (True, 0, 4096),
-    (True, 4096, 2048),
-    (True, 6144, 1024),
-    (True, 7168, 1024),
+    (True, 4096, 3072),
+    (True, 7168, 512),
+    (True, 7680, 512),
 )
 GRAD_PIECES = 8
 GRAD_ROWS = TOK // GRAD_PIECES

time: 53.4 us -> 53.3 us (level)
  no operation moved by 1% of the time
where the time goes in v6:
time: 53.3 us; the launch traced here: 53.2 us
  Pallas kernels  52.6 us (99%)
  between operations  0.64 us (1%)
    pallas_call x1, Pallas kernels, per_device(): pl.pallas_call(kernel, out_shape=[V((HALF, COLS), BF), V((TOK, FEAT), BF)...  51.2 us
    pallas_call x1, Pallas kernels, hand_over(): pl.pallas_call(copies, out_shape=[jax.ShapeDtypeStruct(r.shape, r.dtype)...  1.4 us

profile of v6, /device:TPU:64, one launch (start us, length us, event | category | flops | bytes accessed | tf_op | source)
XLA Modules:
  0.0 53.2 jit_solution(1504837977135132557)
XLA Ops:
  0.6 51.2 %relay_tick.1 = (bf16[64,512]{1,0:T(8,128)(2,1)S(1)}, bf16[128,8192]{1,0:T(8,128)(2,1)S(1)}, f32[1,512]{1,0:T(1,128)S(1)}, f32[16,64]{1,0:T(8,128)S(1)}, f32[64,256]{1,0:T(8,128)S(1)}) custom-call(bf16[128,8192]{1,0:T(8,128)(2,1)} %bitcast.18, bf16[128,8192]{1,0:T(8,128)(2,1)} %bitcast.19, bf16[128,8192]{1,0:T(8,128)(2,1)} %bitcast.20, ...), custom_call_target="tpu_custom_call" | custom-call | tf_op jit(solution)/shard_map/relay_tick/pallas_call | solution.py:449
  51.8 1.4 %hand_over.1 = (bf16[64,512]{1,0:T(8,128)(2,1)}, bf16[128,8192]{1,0:T(8,128)(2,1)}, f32[1,512]{1,0:T(1,128)}, f32[16,64]{1,0:T(8,128)}, f32[64,256]{1,0:T(8,128)}) custom-call(bf16[64,512]{1,0:T(8,128)(2,1)S(1)} %get-tuple-element.15.refs_0_, bf16[128,8192]{1,0:T(8,128)(2,1)S(1)} %get-tuple-element.16.refs_1_, f32[1,512]{1,0:T(1,128)S(1)} %get-tuple-element.17.refs_2_, ...), custom_call_target="tpu_custom_call" | custom-call | tf_op jit(solution)/shard_map/hand_over/pallas_call | solution.py:432
